TPU v7x, 256 devices: a whole 4x4x8 slice. The times are simulated.
256 devices in a mesh: patch: 64 (over y, z, core), sample: 4 (over x).
Axes of the slice: x: 4, y: 4, z: 8, core: 2. Of those that a mesh axis runs over, the one named last changes fastest.
Arguments:
- edge_latents: bfloat16 [4, 65536, 512], P('sample', 'patch'), may hold values from -6 to 6
- node_latents: bfloat16 [4, 16384, 512], P('sample', 'patch'), may hold values from -6 to 6
- edge_cotangent: bfloat16 [4, 65536, 512], P('sample', 'patch'), may hold values from -6 to 6
- node_cotangent: bfloat16 [4, 16384, 512], P('sample', 'patch'), may hold values from -6 to 6
- senders: int32 [65536], P('patch'), may hold values from 0 to 575, as said below
- receivers: int32 [65536], P('patch'), may hold values from 0 to 255
- send_rows: int32 [4096, 4], P('patch'), may hold values from 0 to 255
- edge_first: bfloat16 [1536, 512], replicated, may hold values from -0.15625 to 0.15625
- edge_second: bfloat16 [512, 512], replicated, may hold values from -0.25 to 0.25
- edge_gain: float32 [512], replicated, may hold values from 0.25 to 1.75
- node_first: bfloat16 [1024, 512], replicated, may hold values from -0.1875 to 0.1875
- node_second: bfloat16 [512, 512], replicated, may hold values from -0.25 to 0.25
- node_gain: float32 [512], replicated, may hold values from 0.25 to 1.75
Outputs:
- edge_grad: bfloat16 [4, 65536, 512], P('sample', 'patch')
- node_grad: bfloat16 [4, 16384, 512], P('sample', 'patch')
- edge_first_grad: bfloat16 [1536, 512], replicated
- edge_second_grad: bfloat16 [512, 512], replicated
- node_first_grad: bfloat16 [1024, 512], replicated
- node_second_grad: bfloat16 [512, 512], replicated
- edge_gain_grad: bfloat16 [512], replicated
- node_gain_grad: bfloat16 [512], replicated
Inputs may be any that keep to these rules, and one draw needn't show every extreme that they name: `senders`: each patch's sender table has 576 rows: the last 32 nodes of the patch before it (cyclically), its own 256 nodes, the first 32 nodes of the patch after it, then 4 rows from each patch in order.
All inputs are finite; a program needn't handle non-finite values.
Results may differ from a plain program's by a relative error of at most 0.012.
Values may be sent and summed in bfloat16 or wider, within the bound.
A program may use at most 128 MiB of HBM per device.

v0:
```python
import jax
import jax.numpy as jnp
from jax import lax
from jax.sharding import PartitionSpec as P

RIM = 32
FAR = 4


def with_halo(cells, sides, width):
    for axis, dim in sides:
        count = lax.axis_size(axis)
        head = lax.slice_in_dim(cells, 0, width, axis=dim)
        tail = lax.slice_in_dim(cells, cells.shape[dim] - width, cells.shape[dim], axis=dim)
        cells = jnp.concatenate(
            [
                lax.ppermute(tail, axis, [(i, (i + 1) % count) for i in range(count)]),
                cells,
                lax.ppermute(head, axis, [((i + 1) % count, i) for i in range(count)]),
            ],
            axis=dim,
        )
    return cells


def from_behind(array, axis, by):
    size = lax.axis_size(axis)
    return lax.ppermute(array, axis, [(i, (i + by) % size) for i in range(size)])


def normalize(values):
    center = values - jnp.mean(values, axis=1, keepdims=True)
    spread = jnp.mean(center * center, axis=1, keepdims=True)
    scale = lax.rsqrt(spread + 1e-05)
    return (center * scale, scale)


def normalize_back(grads, normed, scale):
    first = jnp.mean(grads, axis=1, keepdims=True)
    second = jnp.mean(grads * normed, axis=1, keepdims=True)
    return (grads - first - normed * second) * scale


def layer_backward(
    edges_in,
    sent_latent,
    nodes_in,
    recv_ids,
    edge_cot,
    node_cot,
    edge_first,
    edge_second,
    edge_gain,
    node_first,
    node_second,
    node_gain,
):
    width = nodes_in.shape[1]
    recv_latent = nodes_in[recv_ids]
    edge_input = jnp.concatenate([edges_in, sent_latent, recv_latent], axis=1)
    edge_pre = jnp.dot(edge_input, edge_first, preferred_element_type=jnp.float32)
    edge_sig = jax.nn.sigmoid(edge_pre)
    edge_act = (edge_pre * edge_sig).astype(jnp.bfloat16)
    edge_raw = jnp.dot(edge_act, edge_second, preferred_element_type=jnp.float32)
    edge_hat, edge_scale = normalize(edge_raw)
    update = edge_hat * edge_gain
    inflow = jax.ops.segment_sum(update, recv_ids, num_segments=nodes_in.shape[0]).astype(
        jnp.bfloat16
    )
    node_input = jnp.concatenate([nodes_in, inflow], axis=1)
    node_pre = jnp.dot(node_input, node_first, preferred_element_type=jnp.float32)
    node_sig = jax.nn.sigmoid(node_pre)
    node_act = (node_pre * node_sig).astype(jnp.bfloat16)
    node_raw = jnp.dot(node_act, node_second, preferred_element_type=jnp.float32)
    node_hat, node_scale = normalize(node_raw)
    node_upstream = node_cot.astype(jnp.float32)
    node_gain_grad = jnp.sum(node_upstream * node_hat, axis=0)
    node_raw_grad = normalize_back(node_upstream * node_gain, node_hat, node_scale).astype(
        jnp.bfloat16
    )
    node_second_grad = jnp.dot(node_act.T, node_raw_grad, preferred_element_type=jnp.float32)
    node_act_grad = jnp.dot(node_raw_grad, node_second.T, preferred_element_type=jnp.float32)
    node_pre_grad = (node_act_grad * node_sig * (1.0 + node_pre * (1.0 - node_sig))).astype(
        jnp.bfloat16
    )
    node_first_grad = jnp.dot(node_input.T, node_pre_grad, preferred_element_type=jnp.float32)
    node_input_grad = jnp.dot(node_pre_grad, node_first.T, preferred_element_type=jnp.float32)
    update_grad = edge_cot.astype(jnp.float32) + node_input_grad[:, width:][recv_ids]
    edge_gain_grad = jnp.sum(update_grad * edge_hat, axis=0)
    edge_raw_grad = normalize_back(update_grad * edge_gain, edge_hat, edge_scale).astype(
        jnp.bfloat16
    )
    edge_second_grad = jnp.dot(edge_act.T, edge_raw_grad, preferred_element_type=jnp.float32)
    edge_act_grad = jnp.dot(edge_raw_grad, edge_second.T, preferred_element_type=jnp.float32)
    edge_pre_grad = (edge_act_grad * edge_sig * (1.0 + edge_pre * (1.0 - edge_sig))).astype(
        jnp.bfloat16
    )
    edge_first_grad = jnp.dot(edge_input.T, edge_pre_grad, preferred_element_type=jnp.float32)
    edge_input_grad = jnp.dot(edge_pre_grad, edge_first.T, preferred_element_type=jnp.float32)
    edge_grad = (edge_cot.astype(jnp.float32) + edge_input_grad[:, :width]).astype(jnp.bfloat16)
    sent_grad = edge_input_grad[:, width : 2 * width]
    node_partial = (
        node_upstream
        + node_input_grad[:, :width]
        + jax.ops.segment_sum(
            edge_input_grad[:, 2 * width :], recv_ids, num_segments=nodes_in.shape[0]
        )
    )
    weight_terms = (
        edge_first_grad,
        edge_second_grad,
        node_first_grad,
        node_second_grad,
        edge_gain_grad,
        node_gain_grad,
    )
    return (edge_grad, sent_grad, node_partial, weight_terms)


def on_device(
    edge_latents,
    node_latents,
    edge_cotangent,
    node_cotangent,
    senders,
    receivers,
    send_rows,
    edge_first,
    edge_second,
    edge_gain,
    node_first,
    node_second,
    node_gain,
):
    patches = lax.axis_size("patch")
    own_nodes = node_latents[0]
    count = own_nodes.shape[0]
    width = own_nodes.shape[1]
    extended = with_halo(own_nodes, (("patch", 0),), RIM)
    outgoing = own_nodes[send_rows]
    incoming = lax.all_to_all(outgoing, "patch", split_axis=0, concat_axis=0, tiled=True)
    table = jnp.concatenate([extended, incoming.reshape(patches * FAR, width)], axis=0)
    edge_grad, sent_grad, node_partial, weight_terms = layer_backward(
        edge_latents[0],
        table[senders],
        own_nodes,
        receivers,
        edge_cotangent[0],
        node_cotangent[0],
        edge_first,
        edge_second,
        edge_gain,
        node_first,
        node_second,
        node_gain,
    )
    table_grad = jax.ops.segment_sum(sent_grad, senders, num_segments=table.shape[0])
    from_next = from_behind(table_grad[:RIM].astype(jnp.bfloat16), "patch", -1).astype(jnp.float32)
    from_prev = from_behind(
        table_grad[RIM + count : 2 * RIM + count].astype(jnp.bfloat16), "patch", 1
    ).astype(jnp.float32)
    far_grad = table_grad[2 * RIM + count :].reshape(patches, FAR, width)
    returned = lax.all_to_all(
        far_grad.astype(jnp.bfloat16), "patch", split_axis=0, concat_axis=0, tiled=True
    ).astype(far_grad.dtype)
    node_total = node_partial + table_grad[RIM : RIM + count]
    node_total = node_total + jnp.pad(from_prev, ((0, count - RIM), (0, 0)))
    node_total = node_total + jnp.pad(from_next, ((count - RIM, 0), (0, 0)))
    node_total = node_total + jax.ops.segment_sum(
        returned.reshape(patches * FAR, width), send_rows.reshape(-1), num_segments=count
    )
    summed = lax.psum(
        (
            weight_terms[0],
            weight_terms[1],
            weight_terms[2],
            weight_terms[3],
            weight_terms[4],
            weight_terms[5],
        ),
        ("patch", "sample"),
    )
    finals = tuple((term.astype(jnp.bfloat16) for term in summed))
    return (
        edge_grad[None],
        node_total.astype(jnp.bfloat16)[None],
        finals[0],
        finals[1],
        finals[2],
        finals[3],
        finals[4],
        finals[5],
    )


def solution(mesh):
    return jax.shard_map(
        on_device,
        mesh=mesh,
        in_specs=(
            P("sample", "patch", None),
            P("sample", "patch", None),
            P("sample", "patch", None),
            P("sample", "patch", None),
            P("patch"),
            P("patch"),
            P("patch", None),
            P(),
            P(),
            P(),
            P(),
            P(),
            P(),
        ),
        out_specs=(
            P("sample", "patch", None),
            P("sample", "patch", None),
            P(),
            P(),
            P(),
            P(),
            P(),
            P(),
        ),
        check_vma=False,
    )
```

profile of v0, /device:TPU:32, one launch (start us, length us, event | category | flops | bytes accessed | tf_op | source)
XLA Modules:
  0.0 275.9 jit_solution(2588927336006680791)
XLA Ops:
  0.6 0.0 copy-start
  0.7 0.0 copy-start.1
  0.7 0.8 compare_select_fusion.2
  1.5 0.1 copy.26
  1.6 0.1 reshape.84
  1.7 2.2 gather_fusion
  3.9 0.8 reshape.83
  4.7 11.8 %all-to-all-start = ((bf16[64,4,512]{2,1,0:T(4,128)(2,1)}), bf16[64,4,512]{2,1,0:T(4,128)(2,1)S(1)}, u32[]{:S(2)}, u32[]{:S(2)}) async-start(bf16[64,4,512]{2,1,0:T(4,128)(2,1)} %reshape.83), calls=%async_computation | async-start | bytes 524288 | tf_op jit(solution)/shard_map/all_to_all | solution.py:141
  16.5 0.2 collective-permute-start
  16.7 1.6 collective-permute-start.1
  18.3 0.1 copy.30
  18.4 0.6 reshape.140
  19.1 1.5 copy.25
  20.6 5.1 %gather_fusion.2 = bf16[1024,512]{1,0:T(8,128)(2,1)} fusion(bf16[256,512]{1,0:T(8,128)(2,1)S(1)} %bitcast.48, s32[1024]{0:T(1024)S(1)} %fusion.31), kind=kCustom, calls=%fused_computation.2 | custom fusion | bytes 2101248 | tf_op jit(solution)/shard_map/gather | solution.py:59
  25.7 2.8 %all-to-all-done = bf16[64,4,512]{2,1,0:T(4,128)(2,1)S(1)} async-done(((bf16[64,4,512]{2,1,0:T(4,128)(2,1)}), bf16[64,4,512]{2,1,0:T(4,128)(2,1)S(1)}, u32[]{:S(2)}, u32[]{:S(2)}) %all-to-all-start) | async-done | bytes 262176 | tf_op jit(solution)/shard_map/all_to_all | solution.py:141
  28.5 0.8 reshape.75
  29.3 1.0 pad_maximum_fusion.3
  30.3 5.1 %gather_fusion.1 = bf16[1024,512]{1,0:T(8,128)(2,1)} fusion(bf16[576,512]{1,0:T(8,128)(2,1)S(1)} %pad_maximum_fusion.3, s32[1024]{0:T(1024)S(1)} %fusion.30), kind=kCustom, calls=%fused_computation.1 | custom fusion | bytes 2101248 | tf_op jit(solution)/shard_map/gather | solution.py:145
  35.3 5.3 %multiply_convert_fusion.2 = (bf16[1024,512]{1,0:T(8,128)(2,1)S(1)}, f32[1024,512]{1,0:T(8,128)}) fusion(bf16[1536,512]{1,0:T(8,128)(2,1)S(1)} %copy-done, bf16[1024,512]{1,0:T(8,128)(2,1)} %gather_fusion.2, bf16[1024,512]{1,0:T(8,128)(2,1)} %gather_fusion.1, bf16[1024,512]{1,0:T(8,128)(2,1)} %bitcast.52), kind=kOutput, calls=%fused_computation.21 | convolution fusion | flops 1622671360 | bytes 7864320 | tf_op jit(solution)/shard_map/dot_general | solution.py:61
  40.6 0.8 fusion.41
  41.4 0.3 multiply_reduce_fusion.2
  41.7 1.0 copy-done.2
  42.7 1.6 fusion.5
  44.3 2.9 %copy.27 = f32[1024,512]{1,0:T(8,128)} copy(f32[1024,512]{0,1:T(8,128)} %fusion.5) | data formatting | bytes 4194304 | tf_op jit(solution)/shard_map/mul | solution.py:66
  47.2 7.6 %scatter_custom_fusion = f32[256,512]{1,0:T(8,128)S(1)} fusion(s32[1024]{0:T(1024)S(1)} %copy-done.18, f32[1024,512]{1,0:T(8,128)} %copy.27, f32[]{:T(128)} %constant.10.clone.1), kind=kCustom, calls=%fused_computation.59 | custom fusion | flops 524288 | bytes 524800 | tf_op jit(solution)/shard_map/scatter-add | solution.py:67
  54.8 0.0 copy-start.21
  54.8 1.7 fusion.24
  56.6 0.4 fusion.42
  57.0 0.2 multiply_reduce_fusion.4
  57.2 0.3 copy-done.12
  57.5 0.3 fusion.22
  57.8 0.5 fusion.9
  58.3 0.0 copy-start.9
  58.3 1.6 fusion.36
  59.9 0.5 fusion.43
  60.4 1.8 fusion.23
  62.2 4.9 %gather_fusion.3 = f32[1024,512]{1,0:T(8,128)} fusion(f32[256,512]{1,0:T(8,128)S(1)} %slice.63, s32[1024]{0:T(1024)S(1)} %fusion.31), kind=kCustom, calls=%fused_computation.3 | custom fusion | bytes 4198400 | tf_op jit(solution)/shard_map/gather | solution.py:88
  67.1 2.9 %copy.28 = f32[1024,512]{0,1:T(8,128)} copy(f32[1024,512]{1,0:T(8,128)} %gather_fusion.3) | data formatting | bytes 4194304 | tf_op jit(solution)/shard_map/gather | solution.py:88
  70.1 3.2 %multiply_reduce_fusion = (f32[512]{0:T(512)S(1)}, f32[1024]{0:T(1024)S(1)}, f32[1024]{0:T(1024)S(1)}) fusion(f32[1024,512]{0,1:T(8,128)} %copy-done.2, f32[1024]{0:T(1024)S(1)} %add_rsqrt_fusion, f32[1024]{0:T(1024)S(1)} %broadcast_multiply_fusion.2, f32[1024,512]{0,1:T(8,128)} %copy.28, bf16[1,1024,512]{1,2,0:T(8,128)(2,1)S(1)} %copy.25, f32[512]{0:T(512)S(1)} %copy-done.15), kind=kLoop, calls=%fused_computation.16 | loop fusion | flops 5240320 | bytes 5263360 | tf_op jit(solution)/shard_map/reduce_sum | solution.py:89
  73.3 0.3 copy-done.4
  73.5 0.7 multiply_convert_fusion.1
  74.2 0.5 copy-done.11
  74.8 1.7 fusion.45
  76.5 0.0 copy-done.22
  76.6 1.3 multiply_convert_fusion
  77.9 0.2 copy-done.8
  78.1 0.3 copy-done.20
  78.4 3.6 %fusion.6 = f32[1536,512]{1,0:T(8,128)} fusion(bf16[1024,512]{1,0:T(8,128)(2,1)S(1)} %multiply_convert_fusion, bf16[1024,512]{1,0:T(8,128)(2,1)S(1)} %copy-done.7, bf16[1024,512]{1,0:T(8,128)(2,1)S(1)} %copy-done.8, bf16[1024,512]{1,0:T(8,128)(2,1)S(1)} %bitcast.53), kind=kOutput, calls=%fused_computation.26 | convolution fusion | flops 1620049920 | bytes 7340032 | tf_op jit(solution)/shard_map/dot_general | solution.py:98
  82.0 4.5 %fusion.44 = f32[1024,1536]{1,0:T(8,128)} fusion(bf16[1024,512]{1,0:T(8,128)(2,1)S(1)} %multiply_convert_fusion, bf16[1536,512]{1,0:T(8,128)(2,1)S(1)} %copy-done), kind=kOutput, calls=%fused_computation.87 | convolution fusion | flops 1610612736 | bytes 8912896 | tf_op jit(solution)/shard_map/dot_general | solution.py:99
  86.5 8.4 %scatter_custom_fusion.1 = f32[576,512]{1,0:T(8,128)} fusion(s32[1024]{0:T(1024)S(1)} %copy-done.17, f32[1024,1536]{1,0:T(8,128)} %fusion.44, f32[]{:T(128)} %constant.10.clone.1), kind=kCustom, calls=%fused_computation.14 | custom fusion | flops 524288 | bytes 3277312 | tf_op jit(solution)/shard_map/scatter-add | solution.py:157
  94.9 1.3 convert.12
  96.3 3.1 %slice.64 = f32[1024,512]{1,0:T(8,128)} slice(f32[1024,1536]{1,0:T(8,128)} %fusion.44), slice={[0:1024], [0:512]} | slice | bytes 4194304 | tf_op jit(solution)/shard_map/slice | solution.py:100
  99.3 0.8 convert_element_type.83
  100.1 8.7 %all-to-all-start.1 = ((bf16[64,4,512]{2,1,0:T(4,128)(2,1)}), bf16[64,4,512]{2,1,0:T(4,128)(2,1)S(1)}, u32[]{:S(2)}, u32[]{:S(2)}) async-start(bf16[64,4,512]{2,1,0:T(4,128)(2,1)} %convert_element_type.83), calls=%async_computation.1 | async-start | bytes 524288 | tf_op jit(solution)/shard_map/all_to_all | solution.py:163
  108.9 0.2 collective-permute-start.2
  109.1 1.6 collective-permute-start.3
  110.7 3.0 %copy.32 = f32[1024,512]{0,1:T(8,128)} copy(f32[1024,512]{1,0:T(8,128)} %slice.64) | data formatting | bytes 4194304
  113.7 144.9 %all-reduce.4 = (bf16[1536,512]{1,0:T(8,128)(2,1)}, bf16[512,512]{1,0:T(8,128)(2,1)}, bf16[1024,512]{1,0:T(8,128)(2,1)}, bf16[512,512]{1,0:T(8,128)(2,1)}, bf16[512]{0:T(512)(128)(2,1)}, /*index=5*/bf16[512]{0:T(512)(128)(2,1)}) all-reduce(f32[1536,512]{1,0:T(8,128)} %fusion.6, ...), channel_id=1, replica_groups=mesh['patch'=64,'sample'=4] {'patch','sample'}, use_global_device_ids=true, to_apply=%region_12.0 | all-reduce | flops 1836032 | bytes 11016192 | tf_op jit(solution)/shard_map/psum | solution.py:172
  258.6 2.9 %fusion.10 = bf16[1,1024,512]{1,2,0:T(8,128)(2,1)} fusion(f32[1024,512]{0,1:T(8,128)} %copy.32, bf16[1,1024,512]{1,2,0:T(8,128)(2,1)S(1)} %copy.25), kind=kLoop, calls=%fused_computation.31 | loop fusion | flops 1572864 | bytes 4194304 | tf_op jit(solution)/shard_map/broadcast_in_dim | solution.py:185
  261.5 2.4 copy.31
  263.9 1.2 fusion.21
  265.1 7.6 %scatter_custom_fusion.2 = f32[256,512]{1,0:T(8,128)S(1)} fusion(f32[256,512]{1,0:T(8,128)S(1)} %fusion.21, s32[1024]{0:T(1024)S(1)} %copy-done.18, f32[1024,1536]{1,0:T(8,128)} %fusion.44), kind=kCustom, calls=%fused_computation.12 | custom fusion | flops 524288 | bytes 2621440 | tf_op jit(solution)/shard_map/scatter-add | solution.py:105
  272.8 2.3 scatter_custom_fusion.3
  275.1 0.8 fusion.25
  (56 shorter events, 0.3 us)
Async XLA Ops:
  0.6 34.7 %copy-start = (bf16[1536,512]{1,0:T(8,128)(2,1)S(1)}, bf16[1536,512]{1,0:T(8,128)(2,1)}, u32[]{:S(2)}) copy-start(bf16[1536,512]{1,0:T(8,128)(2,1)} %param.20) | copy-start | bytes 4718596
  0.6 17.7 %copy-start.16 = (s32[64,4]{0,1:T(4,128)S(1)}, s32[64,4]{0,1:T(4,128)}, u32[]{:S(2)}) copy-start(s32[64,4]{0,1:T(4,128)} %param.19) | copy-start | bytes 3076
  0.7 15.8 %copy-start.1 = (bf16[1,256,512]{2,1,0:T(8,128)(2,1)S(1)}, bf16[1,256,512]{2,1,0:T(8,128)(2,1)}, u32[]{:S(2)}) copy-start(bf16[1,256,512]{2,1,0:T(8,128)(2,1)} %param.14) | copy-start | bytes 786436
  0.7 17.6 %copy-start.18 = (s32[1024]{0:T(1024)S(1)}, s32[1024]{0:T(1024)}, u32[]{:S(2)}) copy-start(s32[1024]{0:T(1024)} %param.18) | copy-start | bytes 12292
  0.7 17.6 %copy-start.17 = (s32[1024]{0:T(1024)S(1)}, s32[1024]{0:T(1024)}, u32[]{:S(2)}) copy-start(s32[1024]{0:T(1024)} %param.17) | copy-start | bytes 12292
  4.7 23.8 %all-to-all-start = ((bf16[64,4,512]{2,1,0:T(4,128)(2,1)}), bf16[64,4,512]{2,1,0:T(4,128)(2,1)S(1)}, u32[]{:S(2)}, u32[]{:S(2)}) async-start(bf16[64,4,512]{2,1,0:T(4,128)(2,1)} %reshape.83), calls=%async_computation | async-start | bytes 524288 | tf_op jit(solution)/shard_map/all_to_all | solution.py:141
  16.5 12.8 %collective-permute-start = (bf16[32,512]{1,0:T(8,128)(2,1)S(1)}, bf16[32,512]{1,0:T(8,128)(2,1)S(1)}, u32[]{:S(2)}, u32[]{:S(2)}) collective-permute-start(bf16[32,512]{1,0:T(8,128)(2,1)S(1)} %get-tuple-element.38), channel_id=1, source_target_pairs={{0,4},{4,8},{8,12},{12,16},{16,20},{20,24},{24,28},{28,32},{32,36}... | collective-permute-start | bytes 98312 | tf_op jit(solution)/shard_map/ppermute | solution.py:17
  16.7 12.6 %collective-permute-start.1 = (bf16[32,512]{1,0:T(8,128)(2,1)S(1)}, bf16[32,512]{1,0:T(8,128)(2,1)S(1)}, u32[]{:S(2)}, u32[]{:S(2)}) collective-permute-start(bf16[32,512]{1,0:T(8,128)(2,1)S(1)} %get-tuple-element.39), channel_id=1, source_target_pairs={{4,0},{8,4},{12,8},{16,12},{20,16},{24,20},{28,24},{32,28},{36,32}... | collective-permute-start | bytes 98312 | tf_op jit(solution)/shard_map/ppermute | solution.py:19
  35.3 5.3 %copy-start.13 = (bf16[512,512]{1,0:T(8,128)(2,1)S(1)}, bf16[512,512]{1,0:T(8,128)(2,1)}, u32[]{:S(2)}) copy-start(bf16[512,512]{1,0:T(8,128)(2,1)} %param.21) | copy-start | bytes 1572868
  40.6 1.1 copy-start.10
  40.6 2.1 copy-start.15
  41.4 1.3 copy-start.2
  54.8 1.8 copy-start.21
  56.5 1.0 copy-start.12
  56.6 0.9 copy-start.19
  58.3 1.6 copy-start.9
  60.4 1.8 copy-start.5
  70.1 3.2 %copy-start.3 = (f32[1024,512]{0,1:T(8,128)S(1)}, f32[1024,512]{0,1:T(8,128)}, u32[]{:S(2)}) copy-start(f32[1024,512]{0,1:T(8,128)} %copy-done.2) | copy-start | bytes 6291460
  70.1 3.5 %copy-start.4 = (f32[1024,512]{0,1:T(8,128)S(1)}, f32[1024,512]{0,1:T(8,128)}, u32[]{:S(2)}) copy-start(f32[1024,512]{0,1:T(8,128)} %copy.28) | copy-start | bytes 6291460
  73.5 1.2 copy-start.11
  74.8 1.8 copy-start.14
  74.8 1.8 copy-start.22
  76.6 1.3 copy-start.7
  76.6 1.5 copy-start.8
  76.6 1.9 copy-start.20
  100.1 172.6 %all-to-all-start.1 = ((bf16[64,4,512]{2,1,0:T(4,128)(2,1)}), bf16[64,4,512]{2,1,0:T(4,128)(2,1)S(1)}, u32[]{:S(2)}, u32[]{:S(2)}) async-start(bf16[64,4,512]{2,1,0:T(4,128)(2,1)} %convert_element_type.83), calls=%async_computation.1 | async-start | bytes 524288 | tf_op jit(solution)/shard_map/all_to_all | solution.py:163
  108.9 155.0 %collective-permute-start.2 = (bf16[32,512]{1,0:T(8,128)(2,1)S(1)}, bf16[32,512]{1,0:T(8,128)(2,1)S(1)}, u32[]{:S(2)}, u32[]{:S(2)}) collective-permute-start(bf16[32,512]{1,0:T(8,128)(2,1)S(1)} %get-tuple-element.36), channel_id=1, source_target_pairs={{0,4},{4,8},{8,12},{12,16},{16,20},{20,24},{24,28},{28,32},{32,36}... | collective-permute-start | bytes 98312 | tf_op jit(solution)/shard_map/ppermute | solution.py:28
  109.1 154.8 %collective-permute-start.3 = (bf16[32,512]{1,0:T(8,128)(2,1)S(1)}, bf16[32,512]{1,0:T(8,128)(2,1)S(1)}, u32[]{:S(2)}, u32[]{:S(2)}) collective-permute-start(bf16[32,512]{1,0:T(8,128)(2,1)S(1)} %get-tuple-element.37), channel_id=1, source_target_pairs={{0,252},{4,0},{8,4},{12,8},{16,12},{20,16},{24,20},{28,24},{32,28}... | collective-permute-start | bytes 98312 | tf_op jit(solution)/shard_map/ppermute | solution.py:28
  261.5 2.4 copy-start.6
where the time goes:
time: 277 us; the launch traced here: 276 us
  blocking collectives  145 us (52%)
  other arithmetic  40.4 us (15%)
  local copies, waits for them, and re-layouts  39 us (14%)
  starting transfers between devices  24.1 us (9%)
  matrix products  23.5 us (8%)
  waiting for transfers between devices  2.85 us (1%)
    psum x1, blocking collectives, on_device(): lax.psum((weight_terms[0], weight_terms[1], weight_terms[2], weight_terms...  145 us
    all_to_all x1, starting transfers between devices, on_device(): lax.all_to_all(outgoing, 'patch', split_axis=0, concat_axis=0, tiled=True)  11.8 us
    unnamed x50, local copies, waits for them, and re-layouts  9.6 us
    all_to_all x1, starting transfers between devices, on_device(): lax.all_to_all(far_grad.astype(jnp.bfloat16), 'patch', split_axis=0, conc...  8.74 us
    scatter-add x1, other arithmetic, on_device(): jax.ops.segment_sum(sent_grad, senders, num_segments=table.shape[0])  8.43 us
    gather x2, local copies, waits for them, and re-layouts, layer_backward(): node_input_grad[:, width:][recv_ids]  7.83 us
    scatter-add x1, other arithmetic, layer_backward(): jax.ops.segment_sum(edge_input_grad[:, 2 * width:], recv_ids, num_segment...  7.62 us
    scatter-add x1, other arithmetic, layer_backward(): jax.ops.segment_sum(update, recv_ids, num_segments=nodes_in.shape[0])  7.56 us
  transfers between devices with their start and end apart: 6, of which 1 were waited for; matrix products, arithmetic and copies ran while one was open for 9% of the time, Pallas kernels for 0%

commit v1 on v0

--- a/solution.py
+++ b/solution.py
@@ -170,15 +170,18 @@
         returned.reshape(patches * FAR, width), send_rows.reshape(-1), num_segments=count
     )
     summed = lax.psum(
-        (
-            weight_terms[0],
-            weight_terms[1],
-            weight_terms[2],
-            weight_terms[3],
-            weight_terms[4],
-            weight_terms[5],
+        lax.psum(
+            (
+                weight_terms[0],
+                weight_terms[1],
+                weight_terms[2],
+                weight_terms[3],
+                weight_terms[4],
+                weight_terms[5],
+            ),
+            "sample",
         ),
-        ("patch", "sample"),
+        "patch",
     )
     finals = tuple((term.astype(jnp.bfloat16) for term in summed))
     return (

time: 277 us -> 542 us (1.96)
  blocking collectives: 145 us -> 304 us
  waiting for transfers between devices: 2.85 us -> 90.9 us
  between operations: 1.02 us -> 14.4 us
    psum x0 -> x1, blocking collectives: none -> 292 us  [on_device(): lax.psum(lax.psum((weight_terms[0], weight_terms[1], weight_terms[2], wei...]
    psum x1, blocking collectives: 145 us -> 11.7 us  [on_device(): lax.psum((weight_terms[0], weight_terms[1], weight_terms[2], weight_terms...]
    psum x0 -> x1, waiting for transfers between devices: none -> 87.3 us  [on_device(): lax.psum((weight_terms[0], weight_terms[1], weight_terms[2], weight_terms...]
  transfers between devices with their start and end apart: 6 -> 7, of which waited for: 1 -> 2; matrix products, arithmetic and copies ran while one was open for 9% -> 9% of each run, Pallas kernels for 0% -> 0%
where the time goes in v1:
time: 542 us; the launch traced here: 537 us
  blocking collectives  304 us (56%)
  waiting for transfers between devices  90.9 us (17%)
  local copies, waits for them, and re-layouts  40.1 us (7%)
  other arithmetic  39.2 us (7%)
  matrix products  24.7 us (5%)
  starting transfers between devices  23.4 us (4%)
  between operations  14.4 us (3%)
    psum x1, blocking collectives, on_device(): lax.psum(lax.psum((weight_terms[0], weight_terms[1], weight_terms[2], wei...  292 us
    psum x1, waiting for transfers between devices, on_device(): lax.psum((weight_terms[0], weight_terms[1], weight_terms[2], weight_terms...  87.3 us
    all_to_all x1, starting transfers between devices, on_device(): lax.all_to_all(outgoing, 'patch', split_axis=0, concat_axis=0, tiled=True)  11.8 us
    psum x1, blocking collectives, on_device(): lax.psum((weight_terms[0], weight_terms[1], weight_terms[2], weight_terms...  11.7 us
  transfers between devices with their start and end apart: 7, of which 2 were waited for; matrix products, arithmetic and copies ran while one was open for 9% of the time, Pallas kernels for 0%

profile of v1, /device:TPU:32, one launch (start us, length us, event | category | flops | bytes accessed | tf_op | source)
XLA Modules:
  0.0 536.5 jit_solution(5097891553502210984)
XLA Ops:
  7.2 0.8 compare_select_fusion.2
  8.0 0.1 copy.26
  8.1 0.1 reshape.84
  8.2 2.2 gather_fusion
  10.4 0.8 reshape.83
  11.2 11.8 %all-to-all-start = ((bf16[64,4,512]{2,1,0:T(4,128)(2,1)}), bf16[64,4,512]{2,1,0:T(4,128)(2,1)S(1)}, u32[]{:S(2)}, u32[]{:S(2)}) async-start(bf16[64,4,512]{2,1,0:T(4,128)(2,1)} %reshape.83), calls=%async_computation | async-start | bytes 524288 | tf_op jit(solution)/shard_map/all_to_all | solution.py:141
  23.0 0.0 all-reduce.8.cloned.1.call-start
  23.1 0.2 collective-permute-start
  23.3 1.6 collective-permute-start.1
  24.9 1.5 copy.25
  26.4 5.1 gather_fusion.2
  31.5 3.5 all-to-all-done
  35.0 0.8 reshape.75
  35.8 1.0 pad_maximum_fusion.3
  36.8 5.1 gather_fusion.1
  41.9 5.3 multiply_convert_fusion.2
  47.1 0.8 fusion.41
  47.9 0.3 multiply_reduce_fusion.2
  48.3 1.0 copy-done.2
  49.2 1.6 fusion.5
  50.8 2.9 copy.27
  53.7 7.6 %scatter_custom_fusion = f32[256,512]{1,0:T(8,128)S(1)} fusion(s32[1024]{0:T(1024)S(1)} %copy-done.19, f32[1024,512]{1,0:T(8,128)} %copy.27, f32[]{:T(128)} %constant.10.clone.1), kind=kCustom, calls=%fused_computation.59 | custom fusion | flops 524288 | bytes 524800 | tf_op jit(solution)/shard_map/scatter-add | solution.py:67
  61.4 1.7 fusion.24
  63.1 0.4 fusion.42
  63.5 0.2 multiply_reduce_fusion.4
  63.7 0.3 copy-done.13
  64.0 0.3 fusion.22
  64.4 0.5 fusion.9
  64.9 1.5 fusion.36
  66.4 0.5 fusion.43
  66.9 1.8 fusion.23
  68.7 4.9 gather_fusion.3
  73.7 2.9 copy.28
  76.6 3.2 multiply_reduce_fusion
  79.8 0.3 copy-done.4
  80.1 0.7 multiply_convert_fusion.1
  80.8 0.5 copy-done.12
  81.3 1.8 fusion.45
  83.1 0.1 copy-done.25
  83.1 1.3 multiply_convert_fusion
  84.4 1.0 copy-done.24
  85.4 3.5 fusion.6
  88.9 0.0 all-reduce.8.cloned.1.call-update
  88.9 0.7 copy-done.17
  89.6 0.1 copy.30
  89.7 0.7 reshape.140
  90.3 5.7 %fusion.44 = f32[1024,1536]{1,0:T(8,128)} fusion(bf16[1024,512]{1,0:T(8,128)(2,1)} %copy-done.24, bf16[1536,512]{1,0:T(8,128)(2,1)S(1)} %copy-done), kind=kOutput, calls=%fused_computation.87 | convolution fusion | flops 1610612736 | bytes 8912896 | tf_op jit(solution)/shard_map/dot_general | solution.py:99
  96.0 8.4 %scatter_custom_fusion.1 = f32[576,512]{1,0:T(8,128)} fusion(s32[1024]{0:T(1024)S(1)} %copy-done.18, f32[1024,1536]{1,0:T(8,128)} %fusion.44, f32[]{:T(128)} %constant.10.clone.1), kind=kCustom, calls=%fused_computation.14 | custom fusion | flops 524288 | bytes 3277312 | tf_op jit(solution)/shard_map/scatter-add | solution.py:157
  104.5 3.2 slice.64
  107.7 0.1 convert.12
  107.8 0.8 convert_element_type.83
  108.6 8.0 %all-to-all-start.1 = ((bf16[64,4,512]{2,1,0:T(4,128)(2,1)}), bf16[64,4,512]{2,1,0:T(4,128)(2,1)S(1)}, u32[]{:S(2)}, u32[]{:S(2)}) async-start(bf16[64,4,512]{2,1,0:T(4,128)(2,1)} %convert_element_type.83), calls=%async_computation.1 | async-start | bytes 524288 | tf_op jit(solution)/shard_map/all_to_all | solution.py:163
  116.6 0.2 collective-permute-start.2
  116.8 1.6 collective-permute-start.3
  118.4 2.9 copy.32
  121.3 2.9 fusion.10
  124.2 11.7 %all-reduce.3 = (f32[512]{0:T(512)S(1)}, f32[512]{0:T(512)}) all-reduce(f32[512]{0:T(512)S(1)} %get-tuple-element.24, f32[512]{0:T(512)S(1)} %get-tuple-element.27), channel_id=1, replica_groups=mesh['patch'=64,'sample'=4] {'sample'}, use_global_device_ids=true, to_apply=%region_21.22 | all-reduce | flops 1024 | bytes 8192 | tf_op jit(solution)/shard_map/psum | solution.py:173
  135.9 2.3 copy.31
  138.1 1.3 fusion.21
  139.4 7.6 %scatter_custom_fusion.2 = f32[256,512]{1,0:T(8,128)S(1)} fusion(f32[256,512]{1,0:T(8,128)S(1)} %fusion.21, s32[1024]{0:T(1024)S(1)} %copy-done.19, f32[1024,1536]{1,0:T(8,128)} %fusion.44), kind=kCustom, calls=%fused_computation.12 | custom fusion | flops 524288 | bytes 2621440 | tf_op jit(solution)/shard_map/scatter-add | solution.py:105
  147.1 2.3 scatter_custom_fusion.3
  149.5 0.8 fusion.25
  150.2 87.3 %all-reduce.8.cloned.1.call-done = (f32[1536,512]{1,0:T(8,128)}, f32[512,512]{1,0:T(8,128)}, f32[1024,512]{1,0:T(8,128)}, f32[512,512]{1,0:T(8,128)}) async-done(((f32[1536,512]{1,0:T(8,128)}, f32[512,512]{1,0:T(8,128)}, f32[1024,512]{1,0:T(8,128)}, f32[512,512]{1,0:T(8,128)}), (f32[1536,512]{1,0:T(8,128)}, f32[512,512]{1,0:T(8,128)}, f32[1024,512]{1,0:T(8,128)}, ...) | async-done | bytes 7340048 | tf_op jit(solution)/shard_map/psum | solution.py:173
  237.6 292.1 %all-reduce.9 = (bf16[1536,512]{1,0:T(8,128)(2,1)}, bf16[512,512]{1,0:T(8,128)(2,1)}, bf16[1024,512]{1,0:T(8,128)(2,1)}, bf16[512,512]{1,0:T(8,128)(2,1)}, bf16[512]{0:T(512)(128)(2,1)}, /*index=5*/bf16[512]{0:T(512)(128)(2,1)}) all-reduce(f32[1536,512]{1,0:T(8,128)} %get-tuple-element.38, ...), channel_id=1, replica_groups=mesh['patch'=64,'sample'=4] {'patch'}, use_global_device_ids=true, to_apply=%region_13.14 | all-reduce | flops 1836032 | bytes 11016192 | tf_op jit(solution)/shard_map/psum | solution.py:172
  (66 shorter events, 0.3 us)
Async XLA Ops:
  7.2 34.7 %copy-start = (bf16[1536,512]{1,0:T(8,128)(2,1)S(1)}, bf16[1536,512]{1,0:T(8,128)(2,1)}, u32[]{:S(2)}) copy-start(bf16[1536,512]{1,0:T(8,128)(2,1)} %param.20) | copy-start | bytes 4718596
  7.2 15.9 %copy-start.1 = (bf16[1,256,512]{2,1,0:T(8,128)(2,1)S(1)}, bf16[1,256,512]{2,1,0:T(8,128)(2,1)}, u32[]{:S(2)}) copy-start(bf16[1,256,512]{2,1,0:T(8,128)(2,1)} %param.14) | copy-start | bytes 786436
  7.2 17.7 %copy-start.19 = (s32[1024]{0:T(1024)S(1)}, s32[1024]{0:T(1024)}, u32[]{:S(2)}) copy-start(s32[1024]{0:T(1024)} %param.18) | copy-start | bytes 12292
  7.2 17.7 %copy-start.18 = (s32[1024]{0:T(1024)S(1)}, s32[1024]{0:T(1024)}, u32[]{:S(2)}) copy-start(s32[1024]{0:T(1024)} %param.17) | copy-start | bytes 12292
  11.2 23.8 %all-to-all-start = ((bf16[64,4,512]{2,1,0:T(4,128)(2,1)}), bf16[64,4,512]{2,1,0:T(4,128)(2,1)S(1)}, u32[]{:S(2)}, u32[]{:S(2)}) async-start(bf16[64,4,512]{2,1,0:T(4,128)(2,1)} %reshape.83), calls=%async_computation | async-start | bytes 524288 | tf_op jit(solution)/shard_map/all_to_all | solution.py:141
  23.0 214.6 %all-reduce.8.cloned.1.call-start = ((), (), s32[]{:S(2)}) async-start(), calls=%async_computation.2 | async-start | bytes 14680064 | tf_op jit(solution)/shard_map/psum | solution.py:173
  23.1 12.7 %collective-permute-start = (bf16[32,512]{1,0:T(8,128)(2,1)S(1)}, bf16[32,512]{1,0:T(8,128)(2,1)S(1)}, u32[]{:S(2)}, u32[]{:S(2)}) collective-permute-start(bf16[32,512]{1,0:T(8,128)(2,1)S(1)} %get-tuple-element.44), channel_id=1, source_target_pairs={{0,4},{4,8},{8,12},{12,16},{16,20},{20,24},{24,28},{28,32},{32,36}... | collective-permute-start | bytes 98312 | tf_op jit(solution)/shard_map/ppermute | solution.py:17
  23.3 12.5 %collective-permute-start.1 = (bf16[32,512]{1,0:T(8,128)(2,1)S(1)}, bf16[32,512]{1,0:T(8,128)(2,1)S(1)}, u32[]{:S(2)}, u32[]{:S(2)}) collective-permute-start(bf16[32,512]{1,0:T(8,128)(2,1)S(1)} %get-tuple-element.45), channel_id=1, source_target_pairs={{4,0},{8,4},{12,8},{16,12},{20,16},{24,20},{28,24},{32,28},{36,32}... | collective-permute-start | bytes 98312 | tf_op jit(solution)/shard_map/ppermute | solution.py:19
  41.9 5.3 copy-start.14
  47.1 1.1 copy-start.11
  47.1 2.1 copy-start.16
  47.9 1.3 copy-start.2
  61.3 1.8 copy-start.23
  63.1 1.0 copy-start.13
  63.1 0.9 copy-start.20
  64.8 1.6 copy-start.10
  66.9 1.8 copy-start.6
  76.6 3.2 copy-start.3
  76.6 3.5 copy-start.4
  80.1 1.2 copy-start.12
  81.3 1.8 copy-start.15
  81.3 1.8 copy-start.25
  83.1 2.3 copy-start.8
  83.1 2.3 copy-start.9
  83.1 2.3 copy-start.22
  84.4 1.0 copy-start.24
  88.9 0.7 copy-start.17
  104.5 3.2 copy-start.5
  108.6 38.5 %all-to-all-start.1 = ((bf16[64,4,512]{2,1,0:T(4,128)(2,1)}), bf16[64,4,512]{2,1,0:T(4,128)(2,1)S(1)}, u32[]{:S(2)}, u32[]{:S(2)}) async-start(bf16[64,4,512]{2,1,0:T(4,128)(2,1)} %convert_element_type.83), calls=%async_computation.1 | async-start | bytes 524288 | tf_op jit(solution)/shard_map/all_to_all | solution.py:163
  116.6 21.6 %collective-permute-start.2 = (bf16[32,512]{1,0:T(8,128)(2,1)S(1)}, bf16[32,512]{1,0:T(8,128)(2,1)S(1)}, u32[]{:S(2)}, u32[]{:S(2)}) collective-permute-start(bf16[32,512]{1,0:T(8,128)(2,1)S(1)} %get-tuple-element.42), channel_id=1, source_target_pairs={{0,4},{4,8},{8,12},{12,16},{16,20},{20,24},{24,28},{28,32},{32,36}... | collective-permute-start | bytes 98312 | tf_op jit(solution)/shard_map/ppermute | solution.py:28
  116.8 21.4 %collective-permute-start.3 = (bf16[32,512]{1,0:T(8,128)(2,1)S(1)}, bf16[32,512]{1,0:T(8,128)(2,1)S(1)}, u32[]{:S(2)}, u32[]{:S(2)}) collective-permute-start(bf16[32,512]{1,0:T(8,128)(2,1)S(1)} %get-tuple-element.43), channel_id=1, source_target_pairs={{0,252},{4,0},{8,4},{12,8},{16,12},{20,16},{24,20},{28,24},{32,28}... | collective-permute-start | bytes 98312 | tf_op jit(solution)/shard_map/ppermute | solution.py:28
  124.2 13.9 %copy-start.7 = (f32[256,1024]{1,0:T(8,128)S(1)}, f32[256,1024]{1,0:T(8,128)}, u32[]{:S(2)}) copy-start(f32[256,1024]{1,0:T(8,128)} %copy-done.6) | copy-start | bytes 3145732
  139.4 98.2 %copy-start.21 = (f32[512]{0:T(512)S(1)}, f32[512]{0:T(512)}, u32[]{:S(2)}) copy-start(f32[512]{0:T(512)} %get-tuple-element.37) | copy-start | bytes 6148
Sparse Core Ops, SparseCore 0:
  89.0 148.5 all-reduce.7
